TPU v7x, 256 devices: a whole 4x4x8 slice. The times are simulated.
256 devices in a mesh: ctx: 128 (over y, z, x), kvh: 2 (over core).
Axes of the slice: x: 4, y: 4, z: 8, core: 2. Of those that a mesh axis runs over, the one named last changes fastest.
Arguments:
- queries: bfloat16 [32768, 4096], P('ctx', 'kvh'), may hold values from -8 to 8
- current_keys: bfloat16 [32768, 1024], P('ctx', 'kvh'), may hold values from -8 to 8
- current_values: bfloat16 [32768, 1024], P('ctx', 'kvh'), may hold values from -6 to 6
- cached_key_pages: bfloat16 [524288, 1024], P('ctx', 'kvh'), may hold values from -8 to 8
- cached_value_pages: bfloat16 [524288, 1024], P('ctx', 'kvh'), may hold values from -6 to 6
- picks: int32 [128, 32, 3], P('ctx', 'kvh'), may hold values from 0 to 1023, as said below
Outputs:
- attended: bfloat16 [32768, 4096], P('ctx', 'kvh')
Inputs may be any that keep to these rules, and one draw needn't show every extreme that they name: Block n of the cache belongs to owner n // 8. For one query block and one set of 16 consecutive heads (h // 16 fixed), at most 1 of its 48 picks belong to one owner, and for each such set of heads one owner holds exactly 1 picks of every query block. The 3 picks of one query block and head belong to different owners.
All inputs are finite; a program needn't handle non-finite values.
Results may differ from a plain program's by a relative error of at most 0.0055.
Values may be sent and summed in bfloat16 or wider, within the bound.
A program may use at most 128 MiB of HBM per device.

v0:
```python
import functools

import jax
import jax.numpy as jnp
from jax import lax
from jax.experimental import pallas as pl
from jax.experimental.pallas import tpu as pltpu
from jax.sharding import PartitionSpec as P

HEAD_SIZE = 128
KEY_BLOCK_SIZE = 512
TOPK = 3
MESH = pl.DeviceIdType.MESH
NX, NY, NZ = 4, 4, 8
PLANE = NX * NY
HEADS = 16
KV = 4
GROUP = HEADS // KV
OWNED = 8
ROWS = 256
HALF = 128
OWNERS = 128
SCALE = HEAD_SIZE**-0.5
SCALE2 = SCALE * 1.4426950408889634
LOW = -1e30


def kernel(*refs):
    (q_ref, ck_ref, cv_ref, kp_ref, vp_ref, code_ref, csm, out_ref), refs = refs[:8], refs[8:]
    zq, refs = [refs[2 * s : 2 * s + 2] for s in range(NZ)], refs[2 * NZ :]
    ret, refs = [refs[2 * s : 2 * s + 2] for s in range(NZ)], refs[2 * NZ :]
    rl, refs = [refs[2 * s : 2 * s + 2] for s in range(NZ)], refs[2 * NZ :]
    (
        kbuf, vstage, vbuf, tx, rx, lout, zacc, zl, own_o, own_l, pk, pvt, cvt, lt, wt,
        zcode, pcode, zsm, rsm,
        k_sem, v_sem, zq_send, zq_recv, zc_send, zc_recv, pc_send, pc_recv, sm_sem,
        xp_send, xp_recv, tx_send, rx_recv, rs_send, rs_recv, ls_send, ls_recv,
        za_send, za_recv, zl_send, zl_recv,
    ) = refs
    me = lax.axis_index("ctx")
    core = lax.axis_index("kvh")
    x = lax.rem(me, NX)
    z = lax.rem(me // NX, NZ)
    y = me // (NX * NZ)

    def in_plane(k):
        return (
            lax.rem(y + k // NX, NY) * (NX * NZ) + z * NX + lax.rem(x + lax.rem(k, NX), NX),
            core,
        )

    def opposite(k):
        return (
            lax.rem(y + NY - k // NX, NY) * (NX * NZ)
            + z * NX
            + lax.rem(x + NX - lax.rem(k, NX), NX),
            core,
        )

    def along_z(d):
        return (y * (NX * NZ) + lax.rem(z + d + NZ, NZ) * NX + x, core)

    def owner_at(k):
        return in_plane(k)[0]

    def remote(src, dst, send, recv, device):
        return pltpu.make_async_remote_copy(
            src_ref=src,
            dst_ref=dst,
            send_sem=send,
            recv_sem=recv,
            device_id=device,
            device_id_type=MESH,
        )

    def key_copy(v):
        return pltpu.make_async_copy(
            kp_ref.at[:, :, pl.ds(v * HEAD_SIZE, HEAD_SIZE)],
            kbuf.at[pl.ds(v * OWNED, OWNED)],
            k_sem.at[v],
        )

    def value_copy(v):
        return pltpu.make_async_copy(
            vp_ref.at[:, :, pl.ds(v * HEAD_SIZE, HEAD_SIZE)], vstage.at[v % 2], v_sem.at[v]
        )

    value_copy(0).start()
    value_copy(1).start()
    for v in range(KV):
        key_copy(v).start()

    barrier = pltpu.get_barrier_semaphore()
    for k in range(1, PLANE):
        pl.semaphore_signal(barrier, inc=1, device_id=in_plane(k), device_id_type=MESH)
    for d in range(1, NZ):
        pl.semaphore_signal(barrier, inc=1, device_id=along_z(d), device_id_type=MESH)

    for c in range(2):
        for h in range(HEADS):
            zq[0][c][h] = q_ref[
                c * HALF : (c + 1) * HALF, h * HEAD_SIZE : (h + 1) * HEAD_SIZE
            ].T
    for v in range(KV):
        cvt[v] = cv_ref[:, v * HEAD_SIZE : (v + 1) * HEAD_SIZE].T
    zcode[0] = code_ref[...]
    pl.semaphore_wait(barrier, PLANE - 1 + NZ - 1)

    def z_query(s, c, step, part):
        to = (s + step) % NZ
        heads = pl.ds(part * (HEADS // 2), HEADS // 2)
        return remote(
            zq[s][c].at[heads],
            zq[to][c].at[heads],
            zq_send.at[0 if step > 0 else 1, s, c, part],
            zq_recv.at[to, c, part],
            along_z(step),
        )

    def parts_to(s, step):
        return (0, 1) if (s + step) % NZ != NZ // 2 else (0,) if step > 0 else (1,)

    def start_ring(c):
        for part in range(2):
            for step in (1, -1):
                z_query(0, c, step, part).start()

    start_ring(0)

    def z_code(d):
        return remote(zcode.at[0], zcode.at[d], zc_send, zc_recv, along_z(d))

    for d in range(1, NZ):
        z_code(d).start()

    z_codes = remote(
        zcode.at[pl.ds(1, NZ - 1)], zcode.at[pl.ds(1, NZ - 1)], zc_send, zc_recv, along_z(1)
    )
    def query_copy(s, c, k):
        return remote(
            tx.at[s, c, k], rx.at[s, c, k], tx_send.at[s], rx_recv.at[s, c, k], in_plane(k)
        )

    def send_out(s, c):
        def head_for(k):
            owner = owner_at(k)
            return lax.rem(csm[0, owner] if s == 0 else zsm[s, 0, owner], HEADS)

        rx[s, c, 0] = zq[s][c][head_for(0)]

        def body(k, _):
            tx[s, c, k] = zq[s][c][head_for(k)]
            query_copy(s, c, k).start()
            return 0

        lax.fori_loop(1, PLANE, body, 0)

    def pass_on(s, c):
        for step in (1, -1):
            if s == NZ // 2 or (s < NZ // 2) == (step > 0):
                for part in parts_to(s - step, step):
                    z_query((s - step) % NZ, c, step, part).wait_recv()
                    if s != NZ // 2 and part in parts_to(s, step):
                        z_query(s, c, step, part).start()

    def arrive(*pairs):
        for s, c in pairs:
            pass_on(s, c)
        for s, c in pairs:
            send_out(s, c)

    def attend(keys, queries, values):
        scores = jnp.dot(keys, queries, preferred_element_type=jnp.float32)
        top = jnp.max(scores, axis=0, keepdims=True)
        weights = jnp.exp2(scores * SCALE2 - top * SCALE2)
        total = jnp.sum(weights, axis=0, keepdims=True)
        out = jnp.dot(values, weights.astype(jnp.bfloat16), preferred_element_type=jnp.float32)
        return out * (1.0 / total), top * SCALE + jnp.log(total)

    def unit(s, c, k):
        table = lax.div(rsm[k, s, 0, me], HEADS)
        out, level = attend(kbuf[table], rx[s, c, k], vbuf[table])
        rx[s, c, k] = out.astype(jnp.bfloat16)
        lout[s, c, k] = level

    def back_copy(s, c, k):
        return remote(
            rx.at[s, c, k], ret[s][c].at[k], rs_send.at[s], rs_recv.at[s, c], opposite(k)
        )

    def level_copy(s, c, k):
        return remote(
            lout.at[s, c, k], rl[s][c].at[k], ls_send.at[s], ls_recv.at[s, c], opposite(k)
        )

    def units(c, a, b, then=False):
        count = 1 if b is None else 2

        def body(j, _):
            s = a if b is None else a + (b - a) * lax.div(j, PLANE // 4)
            for i in range(4):
                k = lax.rem(j, PLANE // 4) * 4 + i

                def wait(k=k):
                    query_copy(s, c, k).wait_recv()

                if i == 0:
                    pl.when(k > 0)(wait)
                else:
                    wait()
            for i in range(4):
                unit(s, c, lax.rem(j, PLANE // 4) * 4 + i)
            for i in range(4 if then else 0):
                k = lax.rem(j, PLANE // 4) * 4 + i

                def start(k=k):
                    level_copy(s, c, k).start()
                    back_copy(s, c, k).start()

                if i == 0:
                    pl.when(k > 0)(start)
                else:
                    start()
            return 0

        lax.fori_loop(0, count * PLANE // 4, body, 0)
        for s in (a, b)[:count]:
            ret[s][c][0] = rx[s, c, 0]
            rl[s][c][0] = lout[s, c, 0]
            rl[s][c][PLANE] = jnp.full((1, HALF), LOW, jnp.float32)

    def send_back(c, *slots):
        for s in slots:

            def body(k, _, s=s):
                level_copy(s, c, k).start()
                back_copy(s, c, k).start()
                return 0

            lax.fori_loop(1, PLANE, body, 0)

    send_out(0, 0)
    send_out(0, 1)
    odd = lax.rem(me, 2)
    partner = (me + 1 - 2 * odd, core)
    pair = [
        remote(ck_ref, pk, xp_send.at[0], xp_recv.at[0], partner),
        remote(cvt, pvt, xp_send.at[1], xp_recv.at[1], partner),
    ]

    @pl.when(odd == 0)
    def _():
        for copy in pair:
            copy.start()
        pvt[...] = jnp.zeros_like(pvt)


    for v in range(KV):
        value_copy(v).wait()

        def turn(w, _, v=v):
            vbuf[v * OWNED + w] = vstage[v % 2, w].T
            return 0

        lax.fori_loop(0, OWNED, turn, 0)
        if v + 2 < KV:
            value_copy(v + 2).start()

    z_codes.wait_recv()

    def p_code(k):
        return remote(
            zcode.at[:, :, pl.ds(0, OWNERS)], pcode.at[k], pc_send, pc_recv, in_plane(k)
        )

    def start_p_code(k, _):
        p_code(k).start()
        return 0

    lax.fori_loop(1, PLANE, start_p_code, 0)
    pcode[0] = zcode[:, :, :OWNERS]
    z_to_smem = pltpu.make_async_copy(zcode, zsm, sm_sem.at[0])
    z_to_smem.start()
    z_to_smem.wait()

    arrive((1, 0), (7, 0))

    @pl.when(odd == 1)
    def _():
        for copy in pair:
            copy.wait_recv()


    def own(h, _):
        v = h // GROUP
        lanes = pl.ds(pl.multiple_of(v * HEAD_SIZE, HEAD_SIZE), HEAD_SIZE)
        queries = jnp.concatenate([zq[0][0][h], zq[0][1][h]], axis=1)
        before = jnp.dot(pk[:, lanes], queries, preferred_element_type=jnp.float32)
        here = jnp.dot(ck_ref[:, lanes], queries, preferred_element_type=jnp.float32)
        key_pos = lax.broadcasted_iota(jnp.int32, (ROWS, ROWS), 0)
        query_pos = lax.broadcasted_iota(jnp.int32, (ROWS, ROWS), 1)
        before = jnp.where(odd == 1, before, LOW)
        here = jnp.where(key_pos <= query_pos, here, LOW)
        top = jnp.maximum(
            jnp.max(before, axis=0, keepdims=True), jnp.max(here, axis=0, keepdims=True)
        )
        weights_before = jnp.exp2((before - top) * SCALE2)
        weights_here = jnp.exp2((here - top) * SCALE2)
        total = jnp.sum(weights_before, axis=0, keepdims=True) + jnp.sum(
            weights_here, axis=0, keepdims=True
        )
        out = jnp.dot(pvt[v], weights_before.astype(jnp.bfloat16), preferred_element_type=jnp.float32)
        out += jnp.dot(cvt[v], weights_here.astype(jnp.bfloat16), preferred_element_type=jnp.float32)
        out = out * (1.0 / total)
        level = top * SCALE + jnp.log(total)
        for c in range(2):
            own_o[c, h] = out[:, c * HALF : (c + 1) * HALF]
            own_l[c, pl.ds(h, 1), :] = level[:, c * HALF : (c + 1) * HALF]
        return 0

    lax.fori_loop(0, HEADS, own, 0, unroll=2)
    arrive((2, 0), (6, 0))

    remote(
        pcode.at[pl.ds(1, PLANE - 1)], pcode.at[pl.ds(1, PLANE - 1)], pc_send, pc_recv, in_plane(1)
    ).wait_recv()
    p_to_smem = pltpu.make_async_copy(pcode, rsm, sm_sem.at[1])
    p_to_smem.start()
    p_to_smem.wait()
    for v in range(KV):
        key_copy(v).wait()

    units(0, 0, None)
    units(1, 0, None)
    arrive((3, 0), (5, 0))
    start_ring(1)
    units(0, 1, 7)
    arrive((4, 0))
    units(0, 2, 6)
    arrive((1, 1), (7, 1))
    units(0, 4, None, True)
    units(0, 5, None, True)
    units(0, 3, None, True)
    arrive((2, 1), (6, 1))

    def pick(s, h, t):
        owner = zsm[s, 0, OWNERS + h * TOPK + t]
        dx = lax.rem(lax.rem(owner, NX) - x + NX, NX)
        dy = lax.rem(lax.div(owner, NX * NZ) - y + NY, NY)
        dz = lax.rem(lax.rem(lax.div(owner, NX), NZ) - z + NZ, NZ)
        away = lax.div(dz + NZ - 1, NZ)
        return away, (dx + NX * dy) * (1 - away)

    def gather_levels(s, c):
        others = pl.ds(1, PLANE - 1)
        remote(
            rl[s][c].at[others], rl[s][c].at[others], ls_send.at[s], ls_recv.at[s, c], in_plane(1)
        ).wait_recv()

        def body(h, _):
            for t in range(TOPK):
                away, k = pick(s, h, t)
                lt[s, c, t, pl.ds(h, 1), :] = rl[s][c][k + PLANE * away]
            return 0

        lax.fori_loop(0, HEADS, body, 0, unroll=4)

    def weigh(c, heads, levels):
        top = functools.reduce(jnp.maximum, levels)
        parts = [jnp.exp(level - top) for level in levels]
        total = functools.reduce(jnp.add, parts)
        inverse = 1.0 / total
        for i, part in enumerate(parts):
            wt[c, i, heads] = part * inverse
        return top + jnp.log(total)

    def picked_levels(s, c, heads):
        return [lt[s, c, t, heads, :] for t in range(TOPK)]

    def picked_sum(s, c, h):
        total = None
        for t in range(TOPK):
            _, k = pick(s, h, t)
            term = wt[c, t, pl.ds(h, 1), :] * ret[s][c][k].astype(jnp.float32)
            total = term if total is None else total + term
        return total

    def wait_back(s, c):
        remote(
            ret[s][c].at[pl.ds(1, PLANE - 1)], ret[s][c].at[pl.ds(1, PLANE - 1)],
            rs_send.at[s], rs_recv.at[s, c], in_plane(1),
        ).wait_recv()

    def sum_copies(s, c, step):
        to = s + step
        heads = pl.ds(0, HEADS)
        if s == NZ // 2:
            heads = pl.ds(0 if step > 0 else HEADS // 2, HEADS // 2)
        way = 0 if step > 0 else 1
        return [
            remote(
                zacc.at[s, c, heads], zacc.at[to, c, heads], za_send.at[way, s, c],
                za_recv.at[to, c], along_z(step),
            ),
            remote(
                zl.at[s, c, heads], zl.at[to, c, heads], zl_send.at[way, s, c],
                zl_recv.at[to, c], along_z(step),
            ),
        ]

    def steps_from(s):
        return (1, -1) if s == NZ // 2 else (-1,) if s < NZ // 2 else (1,)

    def wait_sum(s, c, step):
        for copy in sum_copies(s - step, c, step):
            copy.wait_recv()

    def combine(c, s):
        gather_levels(s, c)
        wait_back(s, c)
        half = HEADS // 2
        if s == NZ // 2:
            parts = [(0, HEADS, False)]
        elif s == NZ // 2 + 1:
            parts = [(half, half, False), (0, half, True)]
        elif s == NZ // 2 - 1:
            parts = [(0, half, False), (half, half, True)]
        else:
            parts = [(0, HEADS, True)]
        for start, count, upstream in parts:
            heads = slice(start, start + count)
            levels = picked_levels(s, c, heads)
            if upstream:
                wait_sum(s, c, 1 if s > NZ // 2 else -1)
                levels.append(zl[s, c, heads])
            zl[s, c, heads] = weigh(c, heads, levels)

            def body(h, _, upstream=upstream):
                total = picked_sum(s, c, h)
                if upstream:
                    total += wt[c, TOPK, pl.ds(h, 1), :] * zacc[s, c, h].astype(jnp.float32)
                zacc[s, c, h] = total.astype(jnp.bfloat16)
                return 0

            lax.fori_loop(start, start + count, body, 0, unroll=4)
        for step in steps_from(s):
            for copy in sum_copies(s, c, step):
                copy.start()

    combine(0, 4)
    arrive((3, 1), (5, 1))
    arrive((4, 1))
    units(1, 1, 7)
    combine(0, 5)
    combine(0, 3)
    send_back(0, 6, 2)
    units(1, 2, 6)
    units(1, 5, 3)
    units(1, 4, None, True)
    send_back(1, 5, 3)
    combine(0, 6)
    combine(0, 2)
    send_back(0, 7, 1)
    combine(1, 4)
    combine(1, 5)
    combine(1, 3)
    send_back(1, 6, 2)
    combine(0, 7)
    combine(0, 1)
    send_back(1, 7, 1)
    combine(1, 6)
    combine(1, 2)
    send_back(0, 0)
    send_back(1, 0)
    combine(1, 7)
    combine(1, 1)
    for c in range(2):
        gather_levels(0, c)
        wait_back(0, c)
        wait_sum(0, c, -1)
        wait_sum(NZ, c, 1)
        every = slice(0, HEADS)
        weigh(c, every, picked_levels(0, c, every) + [zl[0, c], zl[NZ, c], own_l[c]])

        def finish(h, _, c=c):
            total = picked_sum(0, c, h)
            total += wt[c, TOPK, pl.ds(h, 1), :] * zacc[0, c, h].astype(jnp.float32)
            total += wt[c, TOPK + 1, pl.ds(h, 1), :] * zacc[NZ, c, h].astype(jnp.float32)
            total += wt[c, TOPK + 2, pl.ds(h, 1), :] * own_o[c, h]
            lanes = pl.ds(pl.multiple_of(h * HEAD_SIZE, HEAD_SIZE), HEAD_SIZE)
            out_ref[c * HALF : (c + 1) * HALF, lanes] = total.T.astype(jnp.bfloat16)
            return 0

        lax.fori_loop(0, HEADS, finish, 0, unroll=4)

    z_codes.wait_send()
    remote(
        pcode.at[pl.ds(1, PLANE - 1)], pcode.at[pl.ds(1, PLANE - 1)], pc_send, pc_recv, in_plane(1)
    ).wait_send()

    @pl.when(odd == 0)
    def _():
        for copy in pair:
            copy.wait_send()

    for c in range(2):
        for s in range(NZ):
            for step in (1, -1):
                if s == 0 or (s != NZ // 2 and (s < NZ // 2) == (step > 0)):
                    for part in parts_to(s, step):
                        z_query(s, c, step, part).wait_send()
            if s > 0:
                for step in steps_from(s):
                    for copy in sum_copies(s, c, step):
                        copy.wait_send()
    others = pl.ds(1, PLANE - 1)
    for s in range(NZ):
        remote(
            tx.at[s, :, others], rx.at[s, :, others], tx_send.at[s], rx_recv.at[s, 0, 0], in_plane(1)
        ).wait_send()
        remote(
            rx.at[s, :, others], tx.at[s, :, others], rs_send.at[s], rs_recv.at[s, 0], in_plane(1)
        ).wait_send()
        remote(
            lout.at[s, :, others], lout.at[s, :, others], ls_send.at[s], ls_recv.at[s, 0], in_plane(1)
        ).wait_send()


def exchange(q, ck, cv, kp, vp, code):
    dma = pltpu.SemaphoreType.DMA
    bf16, f32 = jnp.bfloat16, jnp.float32
    half = (HEADS, HEAD_SIZE, HALF)
    scratch = [pltpu.VMEM(half, bf16)] * (2 * NZ)
    scratch += [pltpu.VMEM((PLANE, HEAD_SIZE, HALF), bf16)] * (2 * NZ)
    scratch += [pltpu.VMEM((PLANE + 1, 1, HALF), f32)] * (2 * NZ)
    scratch += [
        pltpu.VMEM((KV * OWNED, KEY_BLOCK_SIZE, HEAD_SIZE), bf16),
        pltpu.VMEM((2, OWNED, KEY_BLOCK_SIZE, HEAD_SIZE), bf16),
        pltpu.VMEM((KV * OWNED, HEAD_SIZE, KEY_BLOCK_SIZE), bf16),
        pltpu.VMEM((NZ, 2, PLANE, HEAD_SIZE, HALF), bf16),
        pltpu.VMEM((NZ, 2, PLANE, HEAD_SIZE, HALF), bf16),
        pltpu.VMEM((NZ, 2, PLANE, 1, HALF), f32),
        pltpu.VMEM((NZ + 1, 2) + half, bf16),
        pltpu.VMEM((NZ + 1, 2, HEADS, HALF), f32),
        pltpu.VMEM((2,) + half, f32),
        pltpu.VMEM((2, HEADS, HALF), f32),
        pltpu.VMEM((ROWS, KV * HEAD_SIZE), bf16),
        pltpu.VMEM((KV, HEAD_SIZE, ROWS), bf16),
        pltpu.VMEM((KV, HEAD_SIZE, ROWS), bf16),
        pltpu.VMEM((NZ, 2, TOPK, HEADS, HALF), f32),
        pltpu.VMEM((2, TOPK + 3, HEADS, HALF), f32),
        pltpu.VMEM((NZ, 1, 2 * OWNERS), jnp.int32),
        pltpu.VMEM((PLANE, NZ, 1, OWNERS), jnp.int32),
        pltpu.SMEM((NZ, 1, 2 * OWNERS), jnp.int32),
        pltpu.SMEM((PLANE, NZ, 1, OWNERS), jnp.int32),
        dma((KV,)), dma((KV,)),
        dma((2, NZ, 2, 2)), dma((NZ, 2, 2)),
        dma, dma, dma, dma, dma((2,)),
        dma((2,)), dma((2,)),
        dma((NZ,)), dma((NZ, 2, PLANE)),
        dma((NZ,)), dma((NZ, 2)),
        dma((NZ,)), dma((NZ, 2)),
        dma((2, NZ, 2)), dma((NZ + 1, 2)), dma((2, NZ, 2)), dma((NZ + 1, 2)),
    ]
    vmem = pl.BlockSpec(memory_space=pltpu.VMEM)
    hbm = pl.BlockSpec(memory_space=pl.ANY)
    return pl.pallas_call(
        kernel,
        out_shape=jax.ShapeDtypeStruct((ROWS, HEADS * HEAD_SIZE), bf16),
        in_specs=[vmem, vmem, vmem, hbm, hbm, vmem, pl.BlockSpec(memory_space=pltpu.SMEM)],
        out_specs=vmem,
        scratch_shapes=scratch,
        compiler_params=pltpu.CompilerParams(
            collective_id=0, has_side_effects=True, vmem_limit_bytes=62 << 20
        ),
        name="attend",
    )(q, ck, cv, kp, vp, code, code)


def local(queries, current_keys, current_values, cached_key_pages, cached_value_pages, picks):
    chosen = picks.reshape(HEADS * TOPK)
    owner = chosen // OWNED
    head = jnp.arange(HEADS * TOPK) // TOPK
    table = head // GROUP * OWNED + chosen % OWNED
    value = head + HEADS * table
    by_owner = jnp.sum(
        jnp.where(owner[None, :] == jnp.arange(OWNERS)[:, None], value[None, :], 0), axis=1
    )
    code = jnp.concatenate([by_owner, jnp.pad(owner, (0, OWNERS - HEADS * TOPK))])
    return exchange(
        queries,
        current_keys,
        current_values,
        cached_key_pages.reshape(OWNED, KEY_BLOCK_SIZE, KV * HEAD_SIZE),
        cached_value_pages.reshape(OWNED, KEY_BLOCK_SIZE, KV * HEAD_SIZE),
        code.reshape(1, 2 * OWNERS).astype(jnp.int32),
    )


def solution(mesh):
    placed = (
        P("ctx", "kvh"),
        P("ctx", "kvh"),
        P("ctx", "kvh"),
        P("ctx", "kvh"),
        P("ctx", "kvh"),
        P("ctx", "kvh", None),
    )
    return jax.shard_map(
        local, mesh=mesh, in_specs=placed, out_specs=P("ctx", "kvh"), check_vma=False
    )
```

profile of v0, /device:TPU:30, one launch (start us, length us, event | category | flops | bytes accessed | tf_op | source)
XLA Modules:
  0.0 219.9 jit_solution(4889809129763452514)
XLA Ops:
  0.0 0.8 copy.9
  0.8 0.1 reshape.95
  0.9 0.1 select_reduce_fusion
  1.0 0.6 pad_add_fusion
  1.5 216.0 %attend.1 = bf16[256,2048]{1,0:T(8,128)(2,1)} custom-call(bf16[256,2048]{1,0:T(8,128)(2,1)} %refs_0_.1, bf16[256,512]{1,0:T(8,128)(2,1)} %refs_1_.1, bf16[256,512]{1,0:T(8,128)(2,1)} %refs_2_.1, bf16[8,512,512]{2,1,0:T(8,128)(2,1)} %bitcast.3, bf16[8,512,512]{2,1,0:T(8,128)(2,1)} %bitcast.4, s32[1,256]{1,0:T(1,128)} %bitcast.5, s32[1,256]{1,0:T(1,128)} %bitcast.6), custom_call_target="tpu_custom_call" | custom-call | tf_op jit(solution)/shard_map/attend/pallas_call | solution.py:567
  217.6 2.3 %copy.11 = bf16[256,2048]{1,0:T(8,128)(2,1)} copy(bf16[256,2048]{1,0:T(8,128)(2,1)} %attend.1) | data formatting | bytes 2097152
  (1 shorter events, 0.0 us)
where the time goes:
time: 220 us
  Pallas kernels  216 us (98%)
  local copies, waits for them, and re-layouts  3.15 us (1%)
    pallas_call x1, Pallas kernels, exchange(): pl.pallas_call(kernel, out_shape=jax.ShapeDtypeStruct((ROWS, HEADS * HEAD...  216 us

commit v1 on v0

--- a/solution.py
+++ b/solution.py
@@ -318,7 +318,7 @@
             own_l[c, pl.ds(h, 1), :] = level[:, c * HALF : (c + 1) * HALF]
         return 0
 
-    lax.fori_loop(0, HEADS, own, 0, unroll=2)
+    lax.fori_loop(0, HEADS, own, 0, unroll=4)
     arrive((2, 0), (6, 0))
 
     remote(
@@ -363,7 +363,7 @@
                 lt[s, c, t, pl.ds(h, 1), :] = rl[s][c][k + PLANE * away]
             return 0
 
-        lax.fori_loop(0, HEADS, body, 0, unroll=4)
+        lax.fori_loop(0, HEADS, body, 0, unroll=16)
 
     def weigh(c, heads, levels):
         top = functools.reduce(jnp.maximum, levels)
@@ -442,7 +442,7 @@
                 zacc[s, c, h] = total.astype(jnp.bfloat16)
                 return 0
 
-            lax.fori_loop(start, start + count, body, 0, unroll=4)
+            lax.fori_loop(start, start + count, body, 0, unroll=8)
         for step in steps_from(s):
             for copy in sum_copies(s, c, step):
                 copy.start()
@@ -491,7 +491,7 @@
             out_ref[c * HALF : (c + 1) * HALF, lanes] = total.T.astype(jnp.bfloat16)
             return 0
 
-        lax.fori_loop(0, HEADS, finish, 0, unroll=4)
+        lax.fori_loop(0, HEADS, finish, 0, unroll=8)
 
     z_codes.wait_send()
     remote(

time: 220 us -> 219 us (level)
  no operation moved by 1% of the time
where the time goes in v1:
time: 219 us
  Pallas kernels  215 us (98%)
  local copies, waits for them, and re-layouts  3.15 us (1%)
    pallas_call x1, Pallas kernels, exchange(): pl.pallas_call(kernel, out_shape=jax.ShapeDtypeStruct((ROWS, HEADS * HEAD...  215 us

profile of v1, /device:TPU:30, one launch (start us, length us, event | category | flops | bytes accessed | tf_op | source)
XLA Modules:
  0.0 219.0 jit_solution(13529528817541242828)
XLA Ops:
  0.0 0.8 copy.9
  0.8 0.1 reshape.95
  0.9 0.1 select_reduce_fusion
  1.0 0.6 pad_add_fusion
  1.5 215.1 %attend.1 = bf16[256,2048]{1,0:T(8,128)(2,1)} custom-call(bf16[256,2048]{1,0:T(8,128)(2,1)} %refs_0_.1, bf16[256,512]{1,0:T(8,128)(2,1)} %refs_1_.1, bf16[256,512]{1,0:T(8,128)(2,1)} %refs_2_.1, bf16[8,512,512]{2,1,0:T(8,128)(2,1)} %bitcast.3, bf16[8,512,512]{2,1,0:T(8,128)(2,1)} %bitcast.4, s32[1,256]{1,0:T(1,128)} %bitcast.5, s32[1,256]{1,0:T(1,128)} %bitcast.6), custom_call_target="tpu_custom_call" | custom-call | tf_op jit(solution)/shard_map/attend/pallas_call | solution.py:567
  216.7 2.3 %copy.11 = bf16[256,2048]{1,0:T(8,128)(2,1)} copy(bf16[256,2048]{1,0:T(8,128)(2,1)} %attend.1) | data formatting | bytes 2097152
  (1 shorter events, 0.0 us)
